TPU v7x, 512 devices: a whole 4x8x8 slice. The times are simulated.
512 devices in a mesh: tensor: 16 (over z_hi, y), dp: 32 (over z_lo, x, core).
Axes of the slice: x: 4, y: 8, z: 8 (z_hi: 2, z_lo: 4; z = z_hi * 4 + z_lo), core: 2. Of those that a mesh axis runs over, the one named last changes fastest.
Arguments:
- tokens: bfloat16 [16384, 4096], P(('dp', 'tensor')), parts along dimension 0, may hold values from -6 to 6
- attn_gain: bfloat16 [4096], replicated, may hold values from 0.5 to 1.5
- query_weight: bfloat16 [4096, 2048], P(None, 'tensor'), may hold values from -1 to 1
- key_value_weight: bfloat16 [4096, 2048], P(None, 'tensor'), may hold values from -1 to 1
- prefix_cache: bfloat16 [131072, 2048], P('dp', 'tensor'), parts along dimension 0, may hold values from -240 to 240, as said below
- out_weight: bfloat16 [2048, 4096], P('tensor'), may hold values from -0.125 to 0.125
- post_gain: bfloat16 [4096], replicated, may hold values from 0.5 to 1.5
Outputs:
- residual_out: bfloat16 [16384, 4096], P(('dp', 'tensor')), parts along dimension 0
- normed_out: bfloat16 [16384, 4096], P(('dp', 'tensor')), parts along dimension 0
There are 32 independent parts, one for each index of `dp`. A program takes and returns all parts, laid end to end along the dimension named above; an argument that names none is the same for every part. Nothing has to cross between parts.
Inputs may be any that keep to these rules, and one draw needn't show every extreme that they name: prefix_cache holds the rotated keys and the values of positions 0 to 4095.
All inputs are finite; a program needn't handle non-finite values.
Results may differ from a plain program's by a relative error of at most 0.04.
Values may be sent and summed in bfloat16 or wider, within the bound.
A program may use at most 64 MiB of HBM per device.

v0:
```python
import jax
import jax.numpy as jnp
from jax import lax
from jax.sharding import PartitionSpec as P

HEAD_SIZE = 128


rope_base = 500000.0
norm_eps = 1e-05


def from_partner(x, axis, distance):
    return lax.ppermute(x, axis, [(i, i ^ 1 << distance) for i in range(lax.axis_size(axis))])


def rms_scale(row_data, gain_vector):
    widened = row_data.astype(jnp.float32)
    mean_square = jnp.mean(widened * widened, axis=-1, keepdims=True)
    return widened * lax.rsqrt(mean_square + norm_eps) * gain_vector.astype(jnp.float32)


def apply_rotation(projected, first_row):
    row_count = projected.shape[0]
    grouped = projected.reshape(row_count, -1, HEAD_SIZE)
    positions = (first_row + jnp.arange(row_count, dtype=jnp.int32)).astype(jnp.float32)
    inverse = rope_base ** (-jnp.arange(HEAD_SIZE // 2, dtype=jnp.float32) * 2.0 / HEAD_SIZE)
    angle_table = positions[:, None] * inverse[None, :]
    cosine = jnp.cos(angle_table)[:, None, :]
    sine_table = jnp.sin(angle_table)[:, None, :]
    lower_half = grouped[..., : HEAD_SIZE // 2]
    upper_half = grouped[..., HEAD_SIZE // 2 :]
    turned = jnp.concatenate(
        [
            lower_half * cosine - upper_half * sine_table,
            upper_half * cosine + lower_half * sine_table,
        ],
        axis=-1,
    )
    return turned.reshape(row_count, -1)


def per_device(
    tokens, attn_gain, query_weight, key_value_weight, prefix_cache, out_weight, post_gain
):
    past_count = prefix_cache.shape[0]
    normalized_input = rms_scale(tokens, attn_gain).astype(jnp.bfloat16)
    keeps_keys = lax.axis_index("tensor") % 2 == 0
    row_block = lax.all_gather(normalized_input, "tensor", axis=0, tiled=True)
    first_row = jnp.int32(0)
    query_part = jnp.dot(row_block, query_weight, preferred_element_type=jnp.float32)
    query_part = apply_rotation(query_part, past_count + first_row).astype(jnp.bfloat16)
    own_part = jnp.dot(row_block, key_value_weight, preferred_element_type=jnp.float32)
    own_part = jnp.where(
        keeps_keys, apply_rotation(own_part, past_count + first_row), own_part
    ).astype(jnp.bfloat16)
    projected = jnp.concatenate([query_part, own_part], axis=1)
    query_width = query_weight.shape[1]
    queries = projected[:, :query_width]
    own_new = projected[:, query_width:]
    own_all = jnp.concatenate([prefix_cache, own_new], axis=0)
    partner_all = from_partner(own_all, "tensor", 0)
    key_row_matrix = jnp.where(keeps_keys, own_all, partner_all)
    value_row_matrix = jnp.where(keeps_keys, partner_all, own_all)
    block_tokens = queries.shape[0]
    query_pos = past_count + jnp.arange(block_tokens, dtype=jnp.int32)
    key_pos = jnp.arange(past_count + block_tokens, dtype=jnp.int32)
    visible = key_pos[None, :] <= query_pos[:, None]
    scores = lax.dot_general(
        queries, key_row_matrix, (((1,), (1,)), ((), ())), preferred_element_type=jnp.float32
    ) * HEAD_SIZE ** (-0.5)
    scores = jnp.where(visible, scores, -1e30)
    row_max = jnp.max(scores, axis=-1, keepdims=True)
    weights = jnp.exp(scores - row_max)
    row_total = jnp.sum(weights, axis=-1, keepdims=True)
    probs = (weights / row_total).astype(jnp.bfloat16)
    outputs = jnp.dot(probs, value_row_matrix, preferred_element_type=jnp.float32).astype(
        jnp.bfloat16
    )
    own_rows = lax.psum_scatter(
        jnp.dot(outputs, out_weight, preferred_element_type=jnp.float32).astype(jnp.bfloat16),
        "tensor",
        scatter_dimension=0,
        tiled=True,
    ).astype(jnp.float32)
    residual_out = (tokens.astype(jnp.float32) + own_rows).astype(jnp.bfloat16)
    normed_out = rms_scale(residual_out, post_gain).astype(jnp.bfloat16)
    return (residual_out, normed_out)


def solution(mesh):
    placed = (
        P(("dp", "tensor"), None),
        P(),
        P(None, "tensor"),
        P(None, "tensor"),
        P("dp", "tensor"),
        P("tensor", None),
        P(),
    )
    return jax.shard_map(
        per_device,
        mesh=mesh,
        in_specs=placed,
        out_specs=(P(("dp", "tensor"), None), P(("dp", "tensor"), None)),
        check_vma=False,
    )
```

profile of v0, /device:TPU:1, one launch (start us, length us, event | category | flops | bytes accessed | tf_op | source)
XLA Modules:
  0.0 440.3 jit_solution(15619498779269705930)
XLA Ops:
  7.2 0.0 copy-start
  7.2 0.0 all-gather.2.cloned.1.call-start
  7.2 0.8 convert_element_type.64
  8.0 1.1 fusion.14
  9.1 1.8 fusion.16
  10.9 0.0 all-gather.2.cloned.1.call-update
  10.9 0.0 reduce-scatter.2.cloned.1.call-start
  11.0 0.0 copy-start.3
  11.0 0.0 copy-start.5
  11.1 135.9 %all-gather.2.cloned.1.call-done = bf16[512,4096]{1,0:T(8,128)(2,1)} async-done(((bf16[32,4096]{1,0:T(8,128)(2,1)}), bf16[512,4096]{1,0:T(8,128)(2,1)}) %all-gather.2.cloned.1.call-update) | async-done | bytes 4194320 | tf_op jit(solution)/shard_map/all_gather | solution.py:49
  146.9 4.0 fusion.40
  150.9 0.6 fusion.32
  151.5 0.1 copy.9
  151.7 0.0 copy-done.3
  151.7 0.1 pad_maximum_fusion
  151.8 2.5 collective-permute-start
  154.2 0.0 copy-done.5
  154.3 3.7 convolution_bitcast_fusion
  158.0 0.6 fusion.29
  158.5 18.4 %collective-permute-done = bf16[4608,128]{1,0:T(8,128)(2,1)S(1)} collective-permute-done((bf16[4608,128]{1,0:T(8,128)(2,1)S(1)}, bf16[4608,128]{1,0:T(8,128)(2,1)S(1)}, u32[]{:S(2)}, u32[]{:S(2)}) %collective-permute-start) | collective-permute-done | bytes 1179680 | tf_op jit(solution)/shard_map/ppermute | solution.py:14
  176.9 0.0 copy-start.7
  176.9 2.6 fusion.39
  179.5 0.0 copy-done.7
  179.5 0.0 copy-start.1
  179.5 3.6 copy-done.1
  183.2 0.0 copy-start.8
  183.2 1.4 fusion
  184.6 0.0 copy-done
  184.6 0.0 copy-done.8
  184.6 10.5 %convolution_convert_fusion = bf16[512,4096]{1,0:T(8,128)(2,1)} fusion(bf16[128,4096]{1,0:T(8,128)(2,1)S(1)} %copy-done, bf16[4608,128]{1,0:T(8,128)(2,1)S(1)} %copy-done.8, pred[]{:T(512)S(6)} %eq.5, f32[512,4608]{1,0:T(8,128)} %copy-done.1, f32[512]{0:T(512)S(1)} %fusion, f32[512]{0:T(512)S(1)} %get-tuple-element.8, bf16[512,128]{1,0:T(8,128)(2,1)S(1)} %copy.9, ...), kind=kOutput, calls=%fused_computation.5 | convolution fusion | flops 1153040384 | bytes 17043456 | tf_op jit(solution)/shard_map/dot_general | solution.py:81
  195.1 0.0 copy-start.6
  195.1 0.0 copy-start.2
  195.1 0.0 reduce-scatter.2.cloned.1.call-update
  195.1 0.7 copy-done.6
  195.8 235.7 %reduce-scatter.2.cloned.1.call-done = bf16[32,4096]{1,0:T(8,128)(2,1)} async-done(((bf16[512,4096]{1,0:T(8,128)(2,1)}), bf16[32,4096]{1,0:T(8,128)(2,1)}) %reduce-scatter.2.cloned.1.call-update) | async-done | bytes 262160 | tf_op jit(solution)/shard_map/reduce_scatter | solution.py:80
  431.5 0.0 copy-done.2
  431.5 1.2 fusion.11
  432.6 0.0 copy-start.4
  432.6 0.8 fusion.13
  433.5 0.0 copy-done.4
  (7 shorter events, 0.1 us)
Async XLA Ops:
  7.2 177.4 %copy-start = (bf16[128,4096]{1,0:T(8,128)(2,1)S(1)}, bf16[128,4096]{1,0:T(8,128)(2,1)}, u32[]{:S(2)}) copy-start(bf16[128,4096]{1,0:T(8,128)(2,1)} %param.12) | copy-start | bytes 3145732
  7.2 139.8 %all-gather.2.cloned.1.call-start = ((), (), s32[]{:S(2)}) async-start(), calls=%async_computation.1 | async-start | bytes 4456448 | tf_op jit(solution)/shard_map/all_gather | solution.py:49
  10.9 420.5 %reduce-scatter.2.cloned.1.call-start = ((), (), s32[]{:S(2)}) async-start(), calls=%async_computation.2 | async-start | bytes 4456448 | tf_op jit(solution)/shard_map/reduce_scatter | solution.py:80
  11.0 140.6 %copy-start.3 = (bf16[4096,128]{1,0:T(8,128)(2,1)S(1)}, bf16[4096,128]{1,0:T(8,128)(2,1)}, u32[]{:S(2)}) copy-start(bf16[4096,128]{1,0:T(8,128)(2,1)} %param.11) | copy-start | bytes 3145732
  11.0 143.2 %copy-start.5 = (bf16[4096,128]{1,0:T(8,128)(2,1)S(1)}, bf16[4096,128]{1,0:T(8,128)(2,1)}, u32[]{:S(2)}) copy-start(bf16[4096,128]{1,0:T(8,128)(2,1)} %param.9) | copy-start | bytes 3145732
  151.8 25.2 %collective-permute-start = (bf16[4608,128]{1,0:T(8,128)(2,1)S(1)}, bf16[4608,128]{1,0:T(8,128)(2,1)S(1)}, u32[]{:S(2)}, u32[]{:S(2)}) collective-permute-start(bf16[4608,128]{1,0:T(8,128)(2,1)S(1)} %pad_maximum_fusion), channel_id=1, source_target_pairs={{0,32},{32,0},{64,96},{96,64},{128,160},{160,128},{192,224},{224,1... | collective-permute-start | bytes 3538952 | tf_op jit(solution)/shard_map/ppermute | solution.py:14
  176.9 2.6 copy-start.7
  179.5 3.6 copy-start.1
  183.2 1.4 copy-start.8
  195.1 0.7 copy-start.6
  195.1 236.4 %copy-start.2 = (bf16[32,4096]{1,0:T(8,128)(2,1)S(1)}, bf16[32,4096]{1,0:T(8,128)(2,1)}, u32[]{:S(2)}) copy-start(bf16[32,4096]{1,0:T(8,128)(2,1)} %param.7) | copy-start | bytes 786436
  432.6 0.9 copy-start.4
Sparse Core Ops, SparseCore 0:
  11.8 135.0 all-gather.1
  195.2 236.2 reduce-scatter.1
where the time goes:
time: 443 us; the launch traced here: 440 us
  waiting for transfers between devices  390 us (88%)
  matrix products  20.8 us (5%)
  between operations  14.2 us (3%)
  other arithmetic  8.33 us (2%)
  local copies, waits for them, and re-layouts  4.43 us (1%)
    reduce_scatter x1, waiting for transfers between devices, per_device(): lax.psum_scatter(jnp.dot(outputs, out_weight, preferred_element_type=jnp....  236 us
    all_gather x1, waiting for transfers between devices, per_device(): row_block = lax.all_gather(normalized_input, 'tensor', axis=0, tiled=True)  136 us
    ppermute x1, waiting for transfers between devices, from_partner(): lax.ppermute(x, axis, [(i, i ^ 1 << distance) for i in range(lax.axis_siz...  18.4 us
    dot_general x1, matrix products, per_device(): jnp.dot(outputs, out_weight, preferred_element_type=jnp.float32)  10.5 us
  transfers between devices with their start and end apart: 3, of which 3 were waited for; matrix products, arithmetic and copies ran while one was open for 1% of the time, Pallas kernels for 0%

commit v1 on v0

v1 whole, which is shorter than its diff:
```python
import functools

import jax
import jax.numpy as jnp
import numpy as np
from jax import lax
from jax.experimental import pallas as pl
from jax.experimental.pallas import tpu as pltpu
from jax.sharding import PartitionSpec as P

MESH = pl.DeviceIdType.MESH
BF16 = jnp.bfloat16
F32 = jnp.float32
HEAD = 128
PAST = 4096
BLOCK = 512
WIDTH = 4096
BASE = 500000.0
EPS = 1e-05
SCALE2 = float(HEAD ** (-0.5) / np.log(2.0))
NEG = -1e30


def rope_tables():
    positions = np.arange(PAST, PAST + BLOCK, dtype=np.float64)
    inverse = BASE ** (-np.arange(HEAD // 2, dtype=np.float64) * 2.0 / HEAD)
    angle = positions[:, None] * inverse[None, :]
    cosine = np.concatenate([np.cos(angle), np.cos(angle)], axis=1)
    sine = np.concatenate([-np.sin(angle), np.sin(angle)], axis=1)
    return cosine.astype(np.float32), sine.astype(np.float32)


def normed(rows, gain):
    mean_square = jnp.mean(rows * rows, axis=-1, keepdims=True)
    return rows * lax.rsqrt(mean_square + EPS) * gain


def kernel(
    tok_h, gain1, wq_h, wkv_h, cache_h, wout_h, gain2, cos_h, sin_h,
    res_o, nrm_o,
    tok, xg, wb, cos_t, sin_t, sres, qb, kvb, wo, att, ar, po, ob,
    m_s, l_s, acc_s,
    ld, xs, xr, wzs, wzr, wxs, wxr, wcs, wcr,
    kfs, kfr, khs, khr, kxs, kxr, qs, qr, ns, nr,
    wys, wyr, zs, zr, zcs, zcr, as_, ar_r, ags, agr, os_, or_,
):
    t = lax.axis_index("tensor")
    d = lax.axis_index("dp")
    zh, y = t // 8, t % 8
    zl, x, c = d // 8, (d // 2) % 4, d % 2
    j, q = y // 2, y % 2
    aligned = c == q
    zi = zh * 4 + zl

    def dev(zh=zh, y=y, zl=zl, x=x, c=c):
        return {"tensor": zh * 8 + y, "dp": zl * 8 + x * 2 + c}

    def remote(src, dst, ss, rs, to):
        return pltpu.make_async_remote_copy(
            src_ref=src, dst_ref=dst, send_sem=ss, recv_sem=rs,
            device_id=to, device_id_type=MESH,
        )

    def arrived(ref, sem):
        pltpu.make_async_copy(ref, ref, sem).wait()

    sib = dev(c=1 - c)
    zmate = dev(zh=1 - zh)
    up, down = dev(y=(y + 1) % 8), dev(y=(y + 7) % 8)

    def zdev(step):
        n = (zi + step) % 8
        return dev(zh=n // 4, zl=n % 4)

    load_tok = pltpu.make_async_copy(tok_h, tok, ld.at[0])
    load_wq = pltpu.make_async_copy(wq_h, wb.at[0, :, pl.ds(0, HEAD)], ld.at[1])
    load_wkv = pltpu.make_async_copy(wkv_h, wb.at[0, :, pl.ds(HEAD, HEAD)], ld.at[2])
    rows_z = pl.ds(pl.multiple_of(zh * 256, 256), 256)
    load_cos = pltpu.make_async_copy(cos_h.at[rows_z], cos_t, ld.at[3])
    load_sin = pltpu.make_async_copy(sin_h.at[rows_z], sin_t, ld.at[4])
    load_tok.start()
    load_wq.start()
    load_wkv.start()

    barrier = pltpu.get_barrier_semaphore()
    mine = t * 2 + c

    def greet(i, carry):
        n = (mine + i) % 32
        pl.semaphore_signal(
            barrier, inc=1,
            device_id={"tensor": n // 2, "dp": zl * 8 + x * 2 + n % 2},
            device_id_type=MESH,
        )
        return carry

    lax.fori_loop(1, 32, greet, 0)
    for i in (1, 2, 3):
        pl.semaphore_signal(barrier, inc=1, device_id=dev(x=(x + i) % 4), device_id_type=MESH)
    for i in (1, 7):
        pl.semaphore_signal(barrier, inc=1, device_id=zdev(i), device_id_type=MESH)
    load_cos.start()
    load_sin.start()

    load_tok.wait()

    def own_rows(n):
        return pl.ds(pl.multiple_of(n * 32, 32), 32)

    xg[own_rows(y), :] = normed(tok[...].astype(F32), gain1[...].astype(F32)).astype(BF16)
    load_wq.wait()
    load_wkv.wait()
    pl.semaphore_wait(barrier, 36)

    def x_copy(step, way, k):
        n = (y - step + 1 + 8) % 8 if way == 0 else (y + step - 1) % 8
        part = xg.at[pl.ds(pl.multiple_of(n * 32 + k * 16, 16), 16), :]
        return remote(part, part, xs.at[way, step - 1, k], xr.at[way, step - 1, k], up if way == 0 else down)

    def x_used(step, way, k):
        return step < 4 or way == k

    for k in range(2):
        for way in range(2):
            x_copy(1, way, k).start()

    def w_rows(xx, cc, k):
        return pl.ds(pl.multiple_of(xx * 1024 + cc * 512 + k * 256, 256), 256)

    def w_z(k):
        r = w_rows(x, c, k)
        return remote(wb.at[0, r], wb.at[1, r], wzs.at[k], wzr.at[k], zmate)

    def w_x(i, k):
        r = w_rows(x, c, k)
        return remote(wb.at[1, r], wb.at[1, r], wxs.at[i - 1, k], wxr.at[i - 1, k], dev(x=(x + i) % 4))

    def w_c(i, k):
        r = w_rows((x + 4 - i) % 4, c, k)
        return remote(wb.at[1, r], wb.at[1, r], wcs.at[i, k], wcr.at[i, k], sib)

    w_z(0).start()
    w_z(1).start()

    def full_local():
        return pltpu.make_async_copy(cache_h, kvb.at[q, pl.ds(0, PAST)], kfr.at[0])

    def full_send():
        return remote(cache_h, kvb.at[q, pl.ds(0, PAST)], kfs.at[0], kfr.at[0], sib)

    def half_rows(h, k):
        return pl.ds(pl.multiple_of(h * 2048 + k * 1024, 1024), 1024)

    def half_send(h, k):
        r = half_rows(h, k)
        return remote(cache_h.at[r], kvb.at[q, r], khs.at[h, k], khr.at[k], dev(y=2 * j + 1 - q, c=h))

    def half_pass(k):
        r = half_rows(c, k)
        return remote(kvb.at[1 - q, r], kvb.at[1 - q, r], kxs.at[k], kxr.at[k], sib)

    @pl.when(aligned)
    def _():
        full_local().start()
        full_send().start()

    def wo_src():
        col = pl.multiple_of((x * 4 + zl) * 256, 256)
        return wout_h.at[:, pl.ds(col, 256)]

    def wo_send(i):
        return remote(wo_src(), wo.at[zl, zh, c, j], wys.at[i], wyr.at[j], dev(y=(y + i) % 8))

    @pl.when(aligned)
    def _():
        pltpu.make_async_copy(wo_src(), wo.at[zl, zh, c, j], wyr.at[j]).start()
        for i in range(1, 8):
            wo_send(i).start()

    def z_copy(step, way):
        n = (zi - step + 1 + 8) % 8 if way == 0 else (zi + step - 1) % 8
        part = wo.at[n % 4, n // 4, c]
        if step == 4:
            part = part.at[pl.ds(2 * way, 2)]
        return remote(part, part, zs.at[way, step - 1], zr.at[way, step - 1], zdev(1 if way == 0 else 7))

    def z_arrived(step):
        for way in range(2):
            z_copy(step, way).wait_recv()

    def z_start(step):
        for way in range(2):
            z_copy(step, way).start()

    def zc_copy(i):
        n = (zi + i) % 8
        part = wo.at[n % 4, n // 4, c]
        return remote(part, part, zcs.at[i], zcr.at[i], sib)

    for step in range(1, 5):
        for k in range(2):
            for way in range(2):
                if x_used(step, way, k):
                    x_copy(step, way, k).wait_recv()
                    if step < 4 and x_used(step + 1, way, k):
                        x_copy(step + 1, way, k).start()
        if step <= 2:
            w_z(step - 1).wait_recv()
            for i in (1, 3, 2):
                w_x(i, step - 1).start()
            w_c(0, step - 1).start()
        if step == 2:
            for i in range(4):
                arrived(wo.at[zl, zh, c, i], wyr.at[i])
            z_start(1)
            zc_copy(0).start()
        if step == 3:
            @pl.when(jnp.logical_not(aligned))
            def _():
                for k in range(2):
                    for h in range(2):
                        half_send(h, k).start()

            for i in (1, 3, 2):
                w_x(i, 0).wait_recv()
                w_c(i, 0).start()
    for i in (1, 3, 2):
        w_x(i, 1).wait_recv()
        w_c(i, 1).start()
    z_arrived(1)
    z_start(2)
    zc_copy(1).start()
    zc_copy(7).start()

    load_cos.wait()
    load_sin.wait()

    def turn(v):
        return v * cos_t[...] + pltpu.roll(v, 64, 1) * sin_t[...]

    def new_rows(z):
        return pl.ds(pl.multiple_of(PAST + z * 256, 256), 256)

    def q_dst():
        return qb.at[rows_z]

    def n_dst():
        return kvb.at[q, new_rows(zh)]

    def q_send(w, to):
        return remote(sres.at[w, 0], q_dst(), qs.at[w], qr.at[zh], to)

    def n_send(w, h, to):
        return remote(sres.at[w, 1], n_dst(), ns.at[w, h], nr.at[q, zh], to)

    def project(w):
        out = jnp.dot(xg[...], wb[w], preferred_element_type=F32)
        part_q, part_n = out[:, :HEAD], out[:, HEAD:]
        sres[w, 0] = turn(part_q).astype(BF16)
        sres[w, 1] = jnp.where(q == 0, turn(part_n), part_n).astype(BF16)

    def spread_own(start):
        @pl.when(aligned)
        def _():
            if start:
                pltpu.make_async_copy(sres.at[0, 0], q_dst(), qr.at[zh]).start()
                pltpu.make_async_copy(sres.at[0, 1], n_dst(), nr.at[q, zh]).start()
                n_send(0, 0, sib).start()
            else:
                n_send(0, 0, sib).wait_send()

        @pl.when(jnp.logical_not(aligned))
        def _():
            copies = [q_send(0, dev(y=2 * j + c, c=q))]
            copies += [n_send(0, h, dev(y=2 * j + c, c=h)) for h in range(2)]
            for copy in copies:
                copy.start() if start else copy.wait_send()

    def spread_other(start):
        copies = [q_send(1, dev(zh=1 - zh, y=2 * j + c, c=q))]
        copies += [n_send(1, h, dev(zh=1 - zh, y=2 * j + c, c=h)) for h in range(2)]
        for copy in copies:
            copy.start() if start else copy.wait_send()

    project(0)
    spread_own(True)
    for k in range(2):
        for i in (0, 1, 3, 2):
            w_c(i, k).wait_recv()
    project(1)
    spread_other(True)

    m_s[...] = jnp.full(m_s.shape, NEG, F32)
    l_s[...] = jnp.zeros(l_s.shape, F32)
    acc_s[...] = jnp.zeros(acc_s.shape, F32)
    z_arrived(2)
    z_start(3)
    zc_copy(2).start()
    zc_copy(6).start()
    for z in range(2):
        arrived(qb.at[pl.ds(0, 256)], qr.at[z])
    arrived(cache_h, kfr.at[0])

    def attend(first, size, masked):
        keys = kvb[0, pl.ds(first, size), :]
        values = kvb[1, pl.ds(first, size), :]
        for tile in range(2):
            rows = pl.ds(tile * 256, 256)
            s = lax.dot_general(qb[rows, :], keys, (((1,), (1,)), ((), ())), preferred_element_type=F32)
            if masked:
                row = lax.broadcasted_iota(jnp.int32, s.shape, 0) + tile * 256
                col = lax.broadcasted_iota(jnp.int32, s.shape, 1)
                s = jnp.where(col <= row, s, NEG)
            old = m_s[rows, :]
            new = jnp.maximum(old, jnp.max(s, axis=1, keepdims=True))
            keep = jnp.exp2((old - new) * SCALE2)
            p = jnp.exp2((s - new[:, :1]) * SCALE2)
            l_s[rows, :] = l_s[rows, :] * keep + jnp.sum(p, axis=1, keepdims=True)
            acc_s[rows, :] = acc_s[rows, :] * keep + jnp.dot(p.astype(BF16), values, preferred_element_type=F32)
            m_s[rows, :] = new

    for k in range(2):
        arrived(kvb.at[0, pl.ds(0, 1024)], khr.at[k])
        half_pass(k).start()
        attend(pl.multiple_of(c * 2048 + k * 1024, 1024), 1024, False)
    z_arrived(3)
    z_start(4)
    zc_copy(3).start()
    zc_copy(5).start()
    for k in range(2):
        half_pass(k).wait_recv()
        attend(pl.multiple_of((1 - c) * 2048 + k * 1024, 1024), 1024, False)
    for kind in range(2):
        for z in range(2):
            arrived(kvb.at[0, pl.ds(0, 256)], nr.at[kind, z])
    attend(PAST, BLOCK, True)
    att[...] = (acc_s[...] / l_s[...]).astype(BF16)

    slot_x = own_rows(x)

    def a_copy(n, remotely):
        src = att.at[own_rows(n)]
        col = pl.multiple_of((zh * 8 + c * 4 + j) * HEAD, HEAD)
        dst = ar.at[slot_x, pl.ds(col, HEAD)]
        sem = ar_r.at[zh * 8 + c * 4 + j]
        if remotely:
            return remote(src, dst, as_.at[n], sem, {"tensor": n, "dp": zl * 8 + x * 2 + q})
        return pltpu.make_async_copy(src, dst, sem)

    def a_start(n, carry):
        stays = jnp.logical_and(n == t, aligned)

        @pl.when(stays)
        def _():
            a_copy(n, False).start()

        @pl.when(jnp.logical_not(stays))
        def _():
            a_copy(n, True).start()

        return carry

    def a_sent(n, carry):
        @pl.when(jnp.logical_not(jnp.logical_and(n == t, aligned)))
        def _():
            a_copy(n, True).wait_send()

        return carry

    lax.fori_loop(0, 16, a_start, 0)
    z_arrived(4)
    zc_copy(4).start()

    def a_here(n, carry):
        arrived(ar.at[pl.ds(0, 32), pl.ds(0, HEAD)], ar_r.at[n])
        return carry

    lax.fori_loop(0, 16, a_here, 0)

    def ag(i):
        return remote(ar.at[slot_x], ar.at[slot_x], ags.at[i - 1], agr.at[i - 1], dev(x=(x + i) % 4))

    for i in (2, 1, 3):
        ag(i).start()
    for i in range(8):
        zc_copy(i).wait_recv()
    for i in (1, 3, 2):
        ag(i).wait_recv()

    def product(n, carry):
        w = wo[n].reshape(2048, 256)
        out = jnp.dot(ar[...], w, preferred_element_type=F32).astype(BF16)
        for i in range(4):
            po[i, n] = out[i * 32 : (i + 1) * 32]
        return carry

    lax.fori_loop(0, 4, product, 0)

    def o_copy(i):
        n = (x + i) % 4
        return remote(po.at[n], ob.at[x], os_.at[i - 1], or_.at[i - 1], dev(x=n))

    for i in (2, 1, 3):
        o_copy(i).start()
    ob[x] = po[x]
    for i in (1, 3, 2):
        o_copy(i).wait_recv()

    total = jnp.zeros((32, 1), F32)
    for n in range(4):
        for k in range(4):
            cols = pl.ds((n * 4 + k) * 256, 256)
            res = (tok[:, cols].astype(F32) + ob[n, k].astype(F32)).astype(BF16)
            res_o[:, cols] = res
            wide = res.astype(F32)
            total = total + jnp.sum(wide * wide, axis=1, keepdims=True)
    scale = lax.rsqrt(total / WIDTH + EPS)
    nrm_o[...] = (res_o[...].astype(F32) * scale * gain2[...].astype(F32)).astype(BF16)

    for step in range(1, 5):
        for k in range(2):
            for way in range(2):
                if x_used(step, way, k):
                    x_copy(step, way, k).wait_send()
        for way in range(2):
            z_copy(step, way).wait_send()
    for k in range(2):
        w_z(k).wait_send()
        half_pass(k).wait_send()
        for i in range(4):
            w_c(i, k).wait_send()
            if i:
                w_x(i, k).wait_send()
    for i in range(8):
        zc_copy(i).wait_send()
    for i in range(1, 4):
        ag(i).wait_send()
        o_copy(i).wait_send()

    @pl.when(aligned)
    def _():
        full_send().wait_send()
        for i in range(1, 8):
            wo_send(i).wait_send()

    @pl.when(jnp.logical_not(aligned))
    def _():
        for k in range(2):
            for h in range(2):
                half_send(h, k).wait_send()

    spread_own(False)
    spread_other(False)
    lax.fori_loop(0, 16, a_sent, 0)


def per_device(tokens, attn_gain, query_weight, key_value_weight, prefix_cache, out_weight, post_gain):
    cosine, sine = rope_tables()
    hbm = pl.BlockSpec(memory_space=pl.ANY)
    vmem = pl.BlockSpec(memory_space=pltpu.VMEM)
    dma = pltpu.SemaphoreType.DMA
    rows = jax.ShapeDtypeStruct(tokens.shape, BF16)
    return pl.pallas_call(
        kernel,
        out_shape=(rows, rows),
        in_specs=[hbm, vmem, hbm, hbm, hbm, hbm, vmem, hbm, hbm],
        out_specs=(vmem, vmem),
        scratch_shapes=[
            pltpu.VMEM((32, WIDTH), BF16),
            pltpu.VMEM((256, WIDTH), BF16),
            pltpu.VMEM((2, WIDTH, 256), BF16),
            pltpu.VMEM((256, HEAD), F32),
            pltpu.VMEM((256, HEAD), F32),
            pltpu.VMEM((2, 2, 256, HEAD), BF16),
            pltpu.VMEM((BLOCK, HEAD), BF16),
            pltpu.VMEM((2, PAST + BLOCK, HEAD), BF16),
            pltpu.VMEM((4, 2, 2, 4, HEAD, 256), BF16),
            pltpu.VMEM((BLOCK, HEAD), BF16),
            pltpu.VMEM((HEAD, 2048), BF16),
            pltpu.VMEM((4, 4, 32, 256), BF16),
            pltpu.VMEM((4, 4, 32, 256), BF16),
            pltpu.VMEM((BLOCK, HEAD), F32),
            pltpu.VMEM((BLOCK, HEAD), F32),
            pltpu.VMEM((BLOCK, HEAD), F32),
            dma((5,)),
            dma((2, 4, 2)), dma((2, 4, 2)),
            dma((2,)), dma((2,)),
            dma((3, 2)), dma((3, 2)),
            dma((4, 2)), dma((4, 2)),
            dma((1,)), dma((1,)),
            dma((2, 2)), dma((2,)),
            dma((2,)), dma((2,)),
            dma((2,)), dma((2,)),
            dma((2, 2)), dma((2, 2)),
            dma((8,)), dma((4,)),
            dma((2, 4)), dma((2, 4)),
            dma((8,)), dma((8,)),
            dma((16,)), dma((16,)),
            dma((3,)), dma((3,)),
            dma((3,)), dma((3,)),
        ],
        compiler_params=pltpu.CompilerParams(
            collective_id=0, has_side_effects=True, vmem_limit_bytes=48 * 2**20
        ),
        name="sublayer",
    )(
        tokens, attn_gain.reshape(1, -1), query_weight, key_value_weight, prefix_cache,
        out_weight, post_gain.reshape(1, -1), jnp.asarray(cosine), jnp.asarray(sine),
    )


def solution(mesh):
    rows = P(("dp", "tensor"), None)
    return jax.shard_map(
        per_device,
        mesh=mesh,
        in_specs=(rows, P(), P(None, "tensor"), P(None, "tensor"), P("dp", "tensor"), P("tensor", None), P()),
        out_specs=(rows, rows),
        check_vma=False,
    )
```

time: 443 us -> 105 us (0.24)
  the two profiles are of different devices: /device:TPU:1 before, /device:TPU:18 now
where the time goes in v1:
time: 105 us
  Pallas kernels  94.3 us (90%)
  local copies, waits for them, and re-layouts  9.88 us (9%)
    pallas_call x1, Pallas kernels, per_device(): pl.pallas_call(kernel, out_shape=(rows, rows), in_specs=[hbm, vmem, hbm,...  94.3 us
    unnamed x18, local copies, waits for them, and re-layouts  9.15 us

profile of v1, /device:TPU:18, one launch (start us, length us, event | category | flops | bytes accessed | tf_op | source)
XLA Modules:
  0.0 104.8 jit_solution(10283999029883617604)
XLA Ops:
  0.6 0.0 copy-start.7
  0.6 0.7 reshape.10.gain1
  1.4 0.0 copy-done.7
  1.4 0.0 copy-start
  1.4 1.2 %copy-done = bf16[4096,128]{1,0:T(8,128)(2,1)S(1)} copy-done((bf16[4096,128]{1,0:T(8,128)(2,1)S(1)}, bf16[4096,128]{1,0:T(8,128)(2,1)}, u32[]{:S(2)}) %copy-start) | copy-done | bytes 1048600
  2.6 0.0 copy-start.1
  2.6 1.2 %copy-done.1 = bf16[4096,128]{1,0:T(8,128)(2,1)S(1)} copy-done((bf16[4096,128]{1,0:T(8,128)(2,1)S(1)}, bf16[4096,128]{1,0:T(8,128)(2,1)}, u32[]{:S(2)}) %copy-start.1) | copy-done | bytes 1048600
  3.8 0.0 copy-start.2
  3.8 1.2 %copy-done.2 = bf16[4096,128]{1,0:T(8,128)(2,1)S(1)} copy-done((bf16[4096,128]{1,0:T(8,128)(2,1)S(1)}, bf16[4096,128]{1,0:T(8,128)(2,1)}, u32[]{:S(2)}) %copy-start.2) | copy-done | bytes 1048600
  5.1 0.0 copy-start.3
  5.1 1.2 %copy-done.3 = bf16[128,4096]{1,0:T(8,128)(2,1)S(1)} copy-done((bf16[128,4096]{1,0:T(8,128)(2,1)S(1)}, bf16[128,4096]{1,0:T(8,128)(2,1)}, u32[]{:S(2)}) %copy-start.3) | copy-done | bytes 1048600
  6.3 0.0 copy-start.4
  6.3 0.9 copy-done.4
  7.2 0.0 copy-start.5
  7.2 0.9 copy-done.5
  8.2 0.0 copy-start.6
  8.2 0.9 copy-done.6
  9.1 94.3 %sublayer.1 = (bf16[32,4096]{1,0:T(8,128)(2,1)S(1)}, bf16[32,4096]{1,0:T(8,128)(2,1)S(1)}) custom-call(bf16[32,4096]{1,0:T(8,128)(2,1)S(1)} %copy-done.4, bf16[1,4096]{1,0:T(2,128)(2,1)S(1)} %reshape.10.gain1, bf16[4096,128]{1,0:T(8,128)(2,1)S(1)} %copy-done, bf16[4096,128]{1,0:T(8,128)(2,1)S(1)} %copy-done.1, bf16[4096,128]{1,0:T(8,128)(2,1)S(1)} %copy-done.2, ...), custom_call_target="tpu_custom_call" | custom-call | tf_op jit(solution)/shard_map/sublayer/pallas_call | solution.py:463
  103.4 0.7 copy.13
  104.1 0.7 copy.14
  (1 shorter events, 0.0 us)
Async XLA Ops:
  0.6 0.7 copy-start.7
  1.4 1.2 %copy-start = (bf16[4096,128]{1,0:T(8,128)(2,1)S(1)}, bf16[4096,128]{1,0:T(8,128)(2,1)}, u32[]{:S(2)}) copy-start(bf16[4096,128]{1,0:T(8,128)(2,1)} %wq_h.1) | copy-start | bytes 3145732
  2.6 1.2 %copy-start.1 = (bf16[4096,128]{1,0:T(8,128)(2,1)S(1)}, bf16[4096,128]{1,0:T(8,128)(2,1)}, u32[]{:S(2)}) copy-start(bf16[4096,128]{1,0:T(8,128)(2,1)} %wkv_h.1) | copy-start | bytes 3145732
  3.8 1.2 %copy-start.2 = (bf16[4096,128]{1,0:T(8,128)(2,1)S(1)}, bf16[4096,128]{1,0:T(8,128)(2,1)}, u32[]{:S(2)}) copy-start(bf16[4096,128]{1,0:T(8,128)(2,1)} %cache_h.1) | copy-start | bytes 3145732
  5.1 1.2 %copy-start.3 = (bf16[128,4096]{1,0:T(8,128)(2,1)S(1)}, bf16[128,4096]{1,0:T(8,128)(2,1)}, u32[]{:S(2)}) copy-start(bf16[128,4096]{1,0:T(8,128)(2,1)} %wout_h.1) | copy-start | bytes 3145732
  6.3 0.9 copy-start.4
  7.2 0.9 copy-start.5
  8.2 0.9 copy-start.6

commit v2 on v1

v2 whole, which is shorter than its diff:
```python
import functools

import jax
import jax.numpy as jnp
import numpy as np
from jax import lax
from jax.experimental import pallas as pl
from jax.experimental.pallas import tpu as pltpu
from jax.sharding import PartitionSpec as P

MESH = pl.DeviceIdType.MESH
BF16 = jnp.bfloat16
F32 = jnp.float32
HEAD = 128
PAST = 4096
BLOCK = 512
WIDTH = 4096
BASE = 500000.0
EPS = 1e-05
SCALE2 = float(HEAD ** (-0.5) / np.log(2.0))
NEG = -1e30


def rope_tables():
    positions = np.arange(PAST, PAST + BLOCK, dtype=np.float64)
    inverse = BASE ** (-np.arange(HEAD // 2, dtype=np.float64) * 2.0 / HEAD)
    angle = positions[:, None] * inverse[None, :]
    cosine = np.concatenate([np.cos(angle), np.cos(angle)], axis=1)
    sine = np.concatenate([-np.sin(angle), np.sin(angle)], axis=1)
    return cosine.astype(np.float32), sine.astype(np.float32)


def normed(rows, gain):
    mean_square = jnp.mean(rows * rows, axis=-1, keepdims=True)
    return rows * lax.rsqrt(mean_square + EPS) * gain


def kernel(
    tok_h, gain1, wq_h, wkv_h, cache_h, wout_h, cos_h, sin_h,
    out_o,
    tok, xg, wb, cos_t, sin_t, sres, qb, kvb, wo, att, ar, po,
    m_s, l_s, acc_s,
    ld, xs, xr, ys, yr, wzs, wzr, wxs, wxr, wcs, wcr,
    kfs, kfr, khs, khr, kxs, kxr, qs, qr, ns, nr, nps,
    zs, zr, zcs, zcr, as_, ar_r, ags, agr, os_, or_,
):
    t = lax.axis_index("tensor")
    d = lax.axis_index("dp")
    zh, y = t // 8, t % 8
    zl, x, c = d // 8, (d // 2) % 4, d % 2
    j, q = y // 2, y % 2
    aligned = c == q
    zi = zh * 4 + zl

    def dev(zh=zh, y=y, zl=zl, x=x, c=c):
        return {"tensor": zh * 8 + y, "dp": zl * 8 + x * 2 + c}

    def remote(src, dst, ss, rs, to):
        return pltpu.make_async_remote_copy(
            src_ref=src, dst_ref=dst, send_sem=ss, recv_sem=rs,
            device_id=to, device_id_type=MESH,
        )

    def arrived(ref, sem):
        pltpu.make_async_copy(ref, ref, sem).wait()

    sib = dev(c=1 - c)
    zmate = dev(zh=1 - zh)
    up, down = dev(y=(y + 1) % 8), dev(y=(y + 7) % 8)

    def zdev(step):
        n = (zi + step) % 8
        return dev(zh=n // 4, zl=n % 4)

    load_tok = pltpu.make_async_copy(tok_h, tok, ld.at[0])
    load_wq = pltpu.make_async_copy(wq_h, wb.at[0, :, pl.ds(0, HEAD)], ld.at[1])
    load_wkv = pltpu.make_async_copy(wkv_h, wb.at[0, :, pl.ds(HEAD, HEAD)], ld.at[2])
    rows_z = pl.ds(pl.multiple_of(zh * 256, 256), 256)
    load_cos = pltpu.make_async_copy(cos_h.at[rows_z], cos_t, ld.at[3])
    load_sin = pltpu.make_async_copy(sin_h.at[rows_z], sin_t, ld.at[4])
    load_tok.start()
    load_wq.start()
    load_wkv.start()

    def wo_piece(n):
        return wo.at[zl, c, zh, n]

    out_col = pl.multiple_of((x * 4 + zl) * 256 + c * HEAD, HEAD)
    load_wo = pltpu.make_async_copy(wout_h.at[:, pl.ds(out_col, HEAD)], wo_piece(y), ld.at[5])

    barrier = pltpu.get_barrier_semaphore()
    greeted = [up, down, zdev(1), zdev(7), zmate, sib, dev(y=2 * j + 1 - q, c=1 - c)]
    greeted += [dev(x=(x + i) % 4) for i in (1, 2, 3)]
    for to in greeted:
        pl.semaphore_signal(barrier, inc=1, device_id=to, device_id_type=MESH)
    load_wo.start()
    load_cos.start()
    load_sin.start()

    load_tok.wait()

    def own_rows(n):
        return pl.ds(pl.multiple_of(n * 32, 32), 32)

    xg[own_rows(y), :] = normed(tok[...].astype(F32), gain1[...].astype(F32).reshape(1, WIDTH)).astype(BF16)
    load_wq.wait()
    load_wkv.wait()
    load_wo.wait()
    pl.semaphore_wait(barrier, len(greeted))

    def x_copy(step, way, k):
        n = (y - step + 1 + 8) % 8 if way == 0 else (y + step - 1) % 8
        part = xg.at[pl.ds(pl.multiple_of(n * 32 + k * 16, 16), 16), :]
        return remote(part, part, xs.at[way, step - 1, k], xr.at[way, step - 1, k], up if way == 0 else down)

    def x_used(step, way, k):
        return step < 4 or way == k

    def y_copy(step, way):
        part = wo_piece((y - step + 1 + 8) % 8 if way == 0 else (y + step - 1) % 8)
        if step == 4:
            part = part.at[pl.ds(64 * way, 64)]
        return remote(part, part, ys.at[way, step - 1], yr.at[way, step - 1], up if way == 0 else down)

    for k in range(2):
        for way in range(2):
            x_copy(1, way, k).start()
    for way in range(2):
        y_copy(1, way).start()

    def w_rows(xx, cc, k):
        return pl.ds(pl.multiple_of(xx * 1024 + cc * 512 + k * 128, 128), 128)

    def w_z(k):
        r = w_rows(x, c, k)
        return remote(wb.at[0, r], wb.at[1, r], wzs.at[k], wzr.at[k], zmate)

    def w_x(i, k):
        r = w_rows(x, c, k)
        return remote(wb.at[1, r], wb.at[1, r], wxs.at[i - 1, k], wxr.at[i - 1, k], dev(x=(x + i) % 4))

    def w_c(i, k):
        r = w_rows((x + 4 - i) % 4, c, k)
        return remote(wb.at[1, r], wb.at[1, r], wcs.at[i, k], wcr.at[i, k], sib)

    for k in range(4):
        w_z(k).start()

    def full_local():
        return pltpu.make_async_copy(cache_h, kvb.at[q, pl.ds(0, PAST)], kfr.at[0])

    def full_send():
        return remote(cache_h, kvb.at[q, pl.ds(0, PAST)], kfs.at[0], kfr.at[0], sib)

    def half_rows(h, k):
        return pl.ds(pl.multiple_of(h * 2048 + k * 1024, 1024), 1024)

    def half_send(h, k):
        r = half_rows(h, k)
        return remote(cache_h.at[r], kvb.at[q, r], khs.at[h, k], khr.at[k], dev(y=2 * j + 1 - q, c=h))

    def half_pass(k):
        r = half_rows(c, k)
        return remote(kvb.at[1 - q, r], kvb.at[1 - q, r], kxs.at[k], kxr.at[k], sib)

    @pl.when(aligned)
    def _():
        full_local().start()
        full_send().start()

    def z_copy(step, way):
        n = (zi - step + 1 + 8) % 8 if way == 0 else (zi + step - 1) % 8
        part = wo.at[n % 4, c, n // 4]
        if step == 4:
            part = part.at[pl.ds(4 * way, 4)]
        return remote(part, part, zs.at[way, step - 1], zr.at[way, step - 1], zdev(1 if way == 0 else 7))

    def z_arrived(step):
        for way in range(2):
            z_copy(step, way).wait_recv()

    def z_start(step):
        for way in range(2):
            z_copy(step, way).start()

    def zc_copy(i):
        n = (zi + i) % 8
        part = wo.at[n % 4, c, n // 4]
        return remote(part, part, zcs.at[i], zcr.at[i], sib)

    for step in range(1, 5):
        for k in range(2):
            for way in range(2):
                if x_used(step, way, k):
                    x_copy(step, way, k).wait_recv()
                    if step < 4 and x_used(step + 1, way, k):
                        x_copy(step + 1, way, k).start()
            n = (step - 1) * 2 + k
            if n < 4:
                w_z(n).wait_recv()
                for i in (2, 1, 3):
                    w_x(i, n).start()
                w_c(0, n).start()
            elif n - 4 < 4:
                for i in (1, 3, 2):
                    w_x(i, n - 4).wait_recv()
                    w_c(i, n - 4).start()
        for way in range(2):
            y_copy(step, way).wait_recv()
            if step < 4:
                y_copy(step + 1, way).start()
        if step == 3:

            @pl.when(jnp.logical_not(aligned))
            def _():
                for h in range(2):
                    half_send(h, 0).start()

    z_start(1)
    zc_copy(0).start()

    load_cos.wait()
    load_sin.wait()

    def turn(v):
        return v * cos_t[...] + pltpu.roll(v, 64, 1) * sin_t[...]

    def new_rows(z):
        return pl.ds(pl.multiple_of(PAST + z * 256, 256), 256)

    def q_dst():
        return qb.at[rows_z]

    def n_dst():
        return kvb.at[q, new_rows(zh)]

    def q_send(w, to):
        return remote(sres.at[w, 0], q_dst(), qs.at[w], qr.at[zh], to)

    def n_send(w, to):
        return remote(sres.at[w, 1], n_dst(), ns.at[w], nr.at[q, zh], to)

    def n_pass(kind, z):
        part = kvb.at[kind, new_rows(z)]
        return remote(part, part, nps.at[kind, z], nr.at[kind, z], sib)

    def project(w):
        out = jnp.dot(xg[...], wb[w], preferred_element_type=F32)
        part_q, part_n = out[:, :HEAD], out[:, HEAD:]
        sres[w, 0] = turn(part_q).astype(BF16)
        sres[w, 1] = jnp.where(q == 0, turn(part_n), part_n).astype(BF16)

    def spread_own(start):
        @pl.when(aligned)
        def _():
            if start:
                pltpu.make_async_copy(sres.at[0, 0], q_dst(), qr.at[zh]).start()
                pltpu.make_async_copy(sres.at[0, 1], n_dst(), nr.at[q, zh]).start()

        @pl.when(jnp.logical_not(aligned))
        def _():
            for copy in (q_send(0, dev(y=2 * j + c, c=q)), n_send(0, dev(y=2 * j + c))):
                copy.start() if start else copy.wait_send()

    def spread_other(start):
        to = functools.partial(dev, zh=1 - zh, y=2 * j + c)
        for copy in (q_send(1, to(c=q)), n_send(1, to())):
            copy.start() if start else copy.wait_send()

    for k in range(4):
        for i in (0, 1, 3, 2):
            w_c(i, k).wait_recv()
    project(1)
    spread_other(True)
    project(0)
    spread_own(True)

    @pl.when(jnp.logical_not(aligned))
    def _():
        for h in range(2):
            half_send(h, 1).start()

    m_s[...] = jnp.full(m_s.shape, NEG, F32)
    l_s[...] = jnp.zeros(l_s.shape, F32)
    acc_s[...] = jnp.zeros(acc_s.shape, F32)
    for z in range(2):
        arrived(qb.at[pl.ds(0, 256)], qr.at[z])
    z_arrived(1)
    z_start(2)
    zc_copy(1).start()
    zc_copy(7).start()
    arrived(cache_h, kfr.at[0])

    def attend(first, size, masked):
        keys = kvb[0, pl.ds(first, size), :]
        values = kvb[1, pl.ds(first, size), :]
        for tile in range(2):
            rows = pl.ds(tile * 256, 256)
            s = lax.dot_general(qb[rows, :], keys, (((1,), (1,)), ((), ())), preferred_element_type=F32)
            if masked:
                row = lax.broadcasted_iota(jnp.int32, s.shape, 0) + tile * 256
                col = lax.broadcasted_iota(jnp.int32, s.shape, 1)
                s = jnp.where(col <= row, s, NEG)
            old = m_s[rows, :]
            new = jnp.maximum(old, jnp.max(s, axis=1, keepdims=True))
            keep = jnp.exp2((old - new) * SCALE2)
            p = jnp.exp2((s - new[:, :1]) * SCALE2)
            l_s[rows, :] = l_s[rows, :] * keep + jnp.sum(p, axis=1, keepdims=True)
            acc_s[rows, :] = acc_s[rows, :] * keep + jnp.dot(p.astype(BF16), values, preferred_element_type=F32)
            m_s[rows, :] = new

    for k in range(2):
        arrived(kvb.at[0, pl.ds(0, 1024)], khr.at[k])
        half_pass(k).start()
        attend(pl.multiple_of(c * 2048 + k * 1024, 1024), 1024, False)
    z_arrived(2)
    z_start(3)
    zc_copy(2).start()
    zc_copy(6).start()

    @pl.when(aligned)
    def _():
        for kind in range(2):
            for z in range(2):
                arrived(kvb.at[0, pl.ds(0, 256)], nr.at[kind, z])
                n_pass(kind, z).start()

    for k in range(2):
        half_pass(k).wait_recv()
        attend(pl.multiple_of((1 - c) * 2048 + k * 1024, 1024), 1024, False)

    @pl.when(jnp.logical_not(aligned))
    def _():
        for kind in range(2):
            for z in range(2):
                arrived(kvb.at[0, pl.ds(0, 256)], nr.at[kind, z])

    attend(PAST, BLOCK, True)
    att[...] = (acc_s[...] / l_s[...]).astype(BF16)

    slot_x = own_rows(x)

    def a_copy(n, remotely):
        src = att.at[own_rows(n)]
        head = zh * 8 + 2 * j + c
        col = pl.multiple_of(head * HEAD, HEAD)
        dst = ar.at[slot_x, pl.ds(col, HEAD)]
        sem = ar_r.at[head]
        if remotely:
            return remote(src, dst, as_.at[n], sem, {"tensor": n, "dp": zl * 8 + x * 2 + q})
        return pltpu.make_async_copy(src, dst, sem)

    def a_start(n, carry):
        stays = jnp.logical_and(n == t, aligned)

        @pl.when(stays)
        def _():
            a_copy(n, False).start()

        @pl.when(jnp.logical_not(stays))
        def _():
            a_copy(n, True).start()

        return carry

    def a_sent(n, carry):
        @pl.when(jnp.logical_not(jnp.logical_and(n == t, aligned)))
        def _():
            a_copy(n, True).wait_send()

        return carry

    lax.fori_loop(0, 16, a_start, 0)
    z_arrived(3)
    z_start(4)
    zc_copy(3).start()
    zc_copy(5).start()

    def a_here(n, carry):
        arrived(ar.at[pl.ds(0, 32), pl.ds(0, HEAD)], ar_r.at[n])
        return carry

    lax.fori_loop(0, 16, a_here, 0)

    def ag(i):
        return remote(ar.at[slot_x], ar.at[slot_x], ags.at[i - 1], agr.at[i - 1], dev(x=(x + i) % 4))

    for i in (2, 1, 3):
        ag(i).start()
    z_arrived(4)
    zc_copy(4).start()
    for i in (1, 3, 2):
        ag(i).wait_recv()
    for i in range(8):
        zc_copy(i).wait_recv()

    def o_copy(i, k):
        n = (x + i) % 4
        dst = out_o.at[:, pl.ds(pl.multiple_of(x * 1024 + k * 512, 512), 512)]
        src = po.at[n, :, pl.ds(k * 512, 512)]
        if i == 0:
            return pltpu.make_async_copy(src, dst, ld.at[6 + k])
        return remote(src, dst, os_.at[i - 1, k], or_.at[i - 1, k], dev(x=n))

    for k in range(2):
        for n in (2 * k, 2 * k + 1):
            w = jnp.concatenate([wo[n, i].reshape(2048, HEAD) for i in range(2)], axis=1)
            out = jnp.dot(ar[...], w, preferred_element_type=F32).astype(BF16)
            for i in range(4):
                po[i, :, n * 256 : (n + 1) * 256] = out[i * 32 : (i + 1) * 32]
        for i in (2, 1, 3, 0):
            o_copy(i, k).start()
    for k in range(2):
        o_copy(0, k).wait()
        for i in (1, 3, 2):
            o_copy(i, k).wait_recv()

    for step in range(1, 5):
        for k in range(2):
            for way in range(2):
                if x_used(step, way, k):
                    x_copy(step, way, k).wait_send()
        for way in range(2):
            y_copy(step, way).wait_send()
            z_copy(step, way).wait_send()
    for k in range(4):
        w_z(k).wait_send()
        for i in range(4):
            w_c(i, k).wait_send()
            if i:
                w_x(i, k).wait_send()
    for i in range(8):
        zc_copy(i).wait_send()
    for k in range(2):
        half_pass(k).wait_send()
        for i in range(1, 4):
            o_copy(i, k).wait_send()
    for i in range(1, 4):
        ag(i).wait_send()

    @pl.when(aligned)
    def _():
        full_send().wait_send()
        for kind in range(2):
            for z in range(2):
                n_pass(kind, z).wait_send()

    @pl.when(jnp.logical_not(aligned))
    def _():
        for k in range(2):
            for h in range(2):
                half_send(h, k).wait_send()

    spread_own(False)
    spread_other(False)
    lax.fori_loop(0, 16, a_sent, 0)


def per_device(tokens, attn_gain, query_weight, key_value_weight, prefix_cache, out_weight, post_gain):
    cosine, sine = rope_tables()
    hbm = pl.BlockSpec(memory_space=pltpu.HBM)
    vmem = pl.BlockSpec(memory_space=pltpu.VMEM)
    dma = pltpu.SemaphoreType.DMA
    attn_sum = pl.pallas_call(
        kernel,
        out_shape=jax.ShapeDtypeStruct(tokens.shape, BF16),
        in_specs=[hbm, vmem, hbm, hbm, hbm, hbm, hbm, hbm],
        out_specs=vmem,
        scratch_shapes=[
            pltpu.VMEM((32, WIDTH), BF16),
            pltpu.VMEM((256, WIDTH), BF16),
            pltpu.VMEM((2, WIDTH, 256), BF16),
            pltpu.VMEM((256, HEAD), F32),
            pltpu.VMEM((256, HEAD), F32),
            pltpu.VMEM((2, 2, 256, HEAD), BF16),
            pltpu.VMEM((BLOCK, HEAD), BF16),
            pltpu.VMEM((2, PAST + BLOCK, HEAD), BF16),
            pltpu.VMEM((4, 2, 2, 8, HEAD, HEAD), BF16),
            pltpu.VMEM((BLOCK, HEAD), BF16),
            pltpu.VMEM((HEAD, 2048), BF16),
            pltpu.VMEM((4, 32, 1024), BF16),
            pltpu.VMEM((BLOCK, HEAD), F32),
            pltpu.VMEM((BLOCK, HEAD), F32),
            pltpu.VMEM((BLOCK, HEAD), F32),
            dma((8,)),
            dma((2, 4, 2)), dma((2, 4, 2)),
            dma((2, 4)), dma((2, 4)),
            dma((4,)), dma((4,)),
            dma((3, 4)), dma((3, 4)),
            dma((4, 4)), dma((4, 4)),
            dma((1,)), dma((1,)),
            dma((2, 2)), dma((2,)),
            dma((2,)), dma((2,)),
            dma((2,)), dma((2,)),
            dma((2,)), dma((2, 2)), dma((2, 2)),
            dma((2, 4)), dma((2, 4)),
            dma((8,)), dma((8,)),
            dma((16,)), dma((16,)),
            dma((3,)), dma((3,)),
            dma((3, 2)), dma((3, 2)),
        ],
        compiler_params=pltpu.CompilerParams(
            collective_id=0, has_side_effects=True, vmem_limit_bytes=60 * 2**20
        ),
        name="sublayer",
    )(
        tokens, attn_gain, query_weight, key_value_weight, prefix_cache,
        out_weight, jnp.asarray(cosine), jnp.asarray(sine),
    )
    residual_out = (tokens.astype(F32) + attn_sum.astype(F32)).astype(BF16)
    gain = post_gain.astype(F32)
    return residual_out, normed(residual_out.astype(F32), gain).astype(BF16)


def solution(mesh):
    rows = P(("dp", "tensor"), None)
    return jax.shard_map(
        per_device,
        mesh=mesh,
        in_specs=(rows, P(), P(None, "tensor"), P(None, "tensor"), P("dp", "tensor"), P("tensor", None), P()),
        out_specs=(rows, rows),
        check_vma=False,
    )
```

time: 105 us -> 91.6 us (0.87)
  the two profiles are of different devices: /device:TPU:18 before, /device:TPU:1 now
where the time goes in v2:
time: 91.6 us; the launch traced here: 91.3 us
  Pallas kernels  88 us (96%)
  other arithmetic  2.69 us (3%)
    pallas_call x1, Pallas kernels, per_device(): pl.pallas_call(kernel, out_shape=jax.ShapeDtypeStruct(tokens.shape, BF16)...  88 us

profile of v2, /device:TPU:1, one launch (start us, length us, event | category | flops | bytes accessed | tf_op | source)
XLA Modules:
  0.0 91.3 jit_solution(6487387754570419759)
XLA Ops:
  0.6 0.7 convert_element_type.22
  1.3 0.0 copy-start
  1.3 88.0 %sublayer.1 = bf16[32,4096]{1,0:T(8,128)(2,1)} custom-call(bf16[32,4096]{1,0:T(8,128)(2,1)} %tok_h.1, bf16[4096]{0:T(1024)(128)(2,1)} %gain1.1, bf16[4096,128]{1,0:T(8,128)(2,1)} %wq_h.1, bf16[4096,128]{1,0:T(8,128)(2,1)} %wkv_h.1, bf16[4096,128]{1,0:T(8,128)(2,1)} %cache_h.1, bf16[128,4096]{1,0:T(8,128)(2,1)} %wout_h.1, f32[512,128]{1,0:T(8,128)} %constant.11.clone.cos_h, ...), custom_call_target="tpu_custom_call" | custom-call | tf_op jit(solution)/shard_map/sublayer/pallas_call | solution.py:464
  89.3 0.0 copy-done
  89.3 1.2 %fusion = (f32[32]{0:T(128)S(1)}, bf16[32,4096]{1,0:T(8,128)(2,1)S(1)}) fusion(bf16[32,4096]{1,0:T(8,128)(2,1)} %sublayer.1, bf16[32,4096]{1,0:T(8,128)(2,1)S(1)} %copy-done), kind=kLoop, calls=%fused_computation.2 | loop fusion | flops 917472 | bytes 786560 | tf_op jit(solution)/shard_map/reduce_sum | solution.py:34
  90.5 0.0 copy-start.1
  90.5 0.8 fusion.2
  91.3 0.0 copy-done.1
  (1 shorter events, 0.0 us)
Async XLA Ops:
  1.3 88.0 %copy-start = (bf16[32,4096]{1,0:T(8,128)(2,1)S(1)}, bf16[32,4096]{1,0:T(8,128)(2,1)}, u32[]{:S(2)}) copy-start(bf16[32,4096]{1,0:T(8,128)(2,1)} %tok_h.1) | copy-start | bytes 786436
  90.5 0.9 copy-start.1

commit v3 on v2

v3 whole, which is shorter than its diff:
```python
import functools

import jax
import jax.numpy as jnp
import numpy as np
from jax import lax
from jax.experimental import pallas as pl
from jax.experimental.pallas import tpu as pltpu
from jax.sharding import PartitionSpec as P

MESH = pl.DeviceIdType.MESH
BF16 = jnp.bfloat16
F32 = jnp.float32
HEAD = 128
PAST = 4096
BLOCK = 512
WIDTH = 4096
BASE = 500000.0
EPS = 1e-05
SCALE2 = float(HEAD ** (-0.5) / np.log(2.0))
NEG = -1e30
Y_AT = (2, 4, 7)
Z_AT = (11, 13)


def rope_tables():
    positions = np.arange(PAST, PAST + BLOCK, dtype=np.float64)
    inverse = BASE ** (-np.arange(HEAD // 2, dtype=np.float64) * 2.0 / HEAD)
    angle = positions[:, None] * inverse[None, :]
    cosine = np.concatenate([np.cos(angle), np.cos(angle)], axis=1)
    sine = np.concatenate([-np.sin(angle), np.sin(angle)], axis=1)
    order = np.arange(BLOCK).reshape(2, 8, 2, 16).transpose(0, 2, 1, 3).reshape(-1)
    cosine, sine = cosine[order], sine[order]
    return cosine.astype(np.float32), sine.astype(np.float32)


def normed(rows, gain):
    mean_square = jnp.mean(rows * rows, axis=-1, keepdims=True)
    return rows * lax.rsqrt(mean_square + EPS) * gain


def kernel(
    tok_h, gain1_h, wq_h, wkv_h, cache_h, wout_h, gain2_h, cos_h, sin_h,
    out_o,
    tok, gain1, gain2, xg, wb, cos_t, sin_t, sres, qb, kvb, wo, att, ar, po, ob,
    m_s, l_s, acc_s,
    ld, xs, xr, ys, yr, wzs, wzr, wxs, wxr, wcs, wcr,
    kfs, kfr, khs, khr, kxs, kxr, qs, qr, ns, nr, nps,
    zs, zr, zcs, zcr, as_, ar_r, ags, agr, os_, or_,
):
    t = lax.axis_index("tensor")
    d = lax.axis_index("dp")
    zh, y = t // 8, t % 8
    zl, x, c = d // 8, (d // 2) % 4, d % 2
    j, q = y // 2, y % 2
    aligned = c == q
    zi = zh * 4 + zl

    def dev(zh=zh, y=y, zl=zl, x=x, c=c):
        return {"tensor": zh * 8 + y, "dp": zl * 8 + x * 2 + c}

    def remote(src, dst, ss, rs, to):
        return pltpu.make_async_remote_copy(
            src_ref=src, dst_ref=dst, send_sem=ss, recv_sem=rs,
            device_id=to, device_id_type=MESH,
        )

    def arrived(ref, sem):
        pltpu.make_async_copy(ref, ref, sem).wait()

    sib = dev(c=1 - c)
    up, down = dev(y=(y + 1) % 8), dev(y=(y + 7) % 8)

    def zdev(step):
        n = (zi + step) % 8
        return dev(zh=n // 4, zl=n % 4)

    load_tok = pltpu.make_async_copy(tok_h, tok, ld.at[0])
    load_wq = pltpu.make_async_copy(wq_h, wb.at[0, :, pl.ds(0, HEAD)], ld.at[1])
    load_wkv = pltpu.make_async_copy(wkv_h, wb.at[0, :, pl.ds(HEAD, HEAD)], ld.at[2])
    rows_z = pl.ds(pl.multiple_of(zh * 256, 256), 256)
    load_cos = pltpu.make_async_copy(cos_h.at[rows_z], cos_t, ld.at[3])
    load_sin = pltpu.make_async_copy(sin_h.at[rows_z], sin_t, ld.at[4])
    load_g1 = pltpu.make_async_copy(gain1_h, gain1, ld.at[6])
    load_g2 = pltpu.make_async_copy(gain2_h, gain2, ld.at[7])
    load_tok.start()
    load_g1.start()
    load_wq.start()
    load_wkv.start()

    def wo_piece(n):
        return wo.at[zl, c, zh, n]

    out_col = pl.multiple_of((x * 4 + zl) * 256 + c * HEAD, HEAD)
    load_wo = pltpu.make_async_copy(wout_h.at[:, pl.ds(out_col, HEAD)], wo_piece(y), ld.at[5])

    barrier = pltpu.get_barrier_semaphore()
    greeted = [up, down, zdev(1), zdev(7), sib, dev(y=2 * j + 1 - q, c=1 - c)]
    greeted += [dev(zh=1 - zh, zl=i) for i in range(4)]
    greeted += [dev(x=(x + i) % 4) for i in (1, 2, 3)]
    for to in greeted:
        pl.semaphore_signal(barrier, inc=1, device_id=to, device_id_type=MESH)
    load_wo.start()
    load_g2.start()
    load_cos.start()
    load_sin.start()

    load_tok.wait()

    load_g1.wait()
    gain = gain1[...].astype(F32).reshape(1, WIDTH)

    def half_of(n, k):
        return pl.ds(pl.multiple_of(k * 128 + n * 16, 16), 16)

    for k in range(2):
        xg[half_of(y, k), :] = normed(tok[pl.ds(k * 16, 16), :].astype(F32), gain).astype(BF16)
    load_wq.wait()
    load_wkv.wait()
    load_wo.wait()
    pl.semaphore_wait(barrier, len(greeted))

    def x_copy(step, way, k, h):
        n = (y - step + 1 + 8) % 8 if way == 0 else (y + step - 1) % 8
        part = xg.at[half_of(n, k), pl.ds(h * 2048, 2048)]
        at = (way, step - 1, k, h)
        return remote(part, part, xs.at[at], xr.at[at], up if way == 0 else down)

    def x_used(step, way, k):
        return step < 4 or way == k

    def y_copy(step, way):
        part = wo_piece((y - step + 1 + 8) % 8 if way == 0 else (y + step - 1) % 8)
        if step == 4:
            part = part.at[pl.ds(64 * way, 64)]
        return remote(part, part, ys.at[way, step - 1], yr.at[way, step - 1], up if way == 0 else down)

    for way in range(2):
        x_copy(1, way, 0, 0).start()
        y_copy(1, way).start()
    for k, h in ((0, 1), (1, 0), (1, 1)):
        for way in range(2):
            x_copy(1, way, k, h).start()

    def w_rows(xx, cc, k):
        return pl.ds(pl.multiple_of(xx * 1024 + cc * 512 + k * 128, 128), 128)

    def w_z(k):
        r = w_rows(x, c, zl)
        return remote(wb.at[0, r], wb.at[1, r], wzs.at[k], wzr.at[zl], dev(zh=1 - zh, zl=k))

    def w_x(way, k):
        r = w_rows(x, c, k)
        return remote(wb.at[1, r], wb.at[1, r], wxs.at[way, k], wxr.at[way, k], dev(x=(x + 1 + 2 * way) % 4))

    def w_far(k):
        way = k // 2
        r = w_rows((x + 3 + 2 * way) % 4, c, k)
        return remote(wb.at[1, r], wb.at[1, r], wxs.at[2, k], wxr.at[2, k], dev(x=(x + 1 + 2 * way) % 4))

    def w_c(i, k):
        r = w_rows((x + 4 - i) % 4, c, k)
        return remote(wb.at[1, r], wb.at[1, r], wcs.at[i, k], wcr.at[i, k], sib)

    for k in range(4):
        w_z(k).start()

    def full_local():
        return pltpu.make_async_copy(cache_h, kvb.at[q, pl.ds(0, PAST)], kfr.at[0])

    def full_send():
        return remote(cache_h, kvb.at[q, pl.ds(0, PAST)], kfs.at[0], kfr.at[0], sib)

    def half_rows(h, k):
        return pl.ds(pl.multiple_of(h * 2048 + k * 1024, 1024), 1024)

    def half_send(h, k):
        r = half_rows(h, k)
        return remote(cache_h.at[r], kvb.at[q, r], khs.at[h, k], khr.at[k], dev(y=2 * j + 1 - q, c=h))

    def half_pass(k):
        r = half_rows(c, k)
        return remote(kvb.at[1 - q, r], kvb.at[1 - q, r], kxs.at[k], kxr.at[k], sib)

    @pl.when(aligned)
    def _():
        full_local().start()
        full_send().start()

    def z_copy(step, way, k):
        n = (zi - step + 1 + 8) % 8 if way == 0 else (zi + step - 1) % 8
        part = wo.at[n % 4, c, n // 4, pl.ds(4 * k, 4)]
        return remote(part, part, zs.at[way, step - 1, k], zr.at[way, step - 1, k], zdev(1 if way == 0 else 7))

    def z_arrived(step, k):
        for way in range(2):
            if x_used(step, way, k):
                z_copy(step, way, k).wait_recv()

    def z_start(step, k):
        for way in range(2):
            if x_used(step, way, k):
                z_copy(step, way, k).start()

    def zc_copy(i):
        n = (zi + i) % 8
        part = wo.at[n % 4, c, n // 4]
        return remote(part, part, zcs.at[i], zcr.at[i], sib)

    def y_next(step):
        for way in range(2):
            y_copy(step, way).wait_recv()
            if step < 4:
                y_copy(step + 1, way).start()

    def z_next(step, k):
        z_arrived(step, k)
        z_start(step + 1, k)

    def z_share(step):
        zc_copy(step).start()
        zc_copy(8 - step).start()

    def weights_in():
        for n in range(4):
            arrived(wb.at[1, w_rows(x, c, n)], wzr.at[n])
            for way in range(2):
                w_x(way, n).start()
            w_c(0, n).start()

    def weights_on(n):
        for way in range(2):
            w_x(way, n).wait_recv()
            if way == n // 2:
                w_far(n).start()
            w_c(1 + 2 * way, n).start()

    def weights_far(n):
        w_far(n).wait_recv()
        w_c(2, n).start()

    def after(event):
        if event in Y_AT:
            y_next(Y_AT.index(event) + 2)
        if event == 5:
            weights_in()
        if event in (8, 9, 10, 11):
            weights_on(event - 8)
        if event == 11:

            @pl.when(jnp.logical_not(aligned))
            def _():
                for k in range(2):
                    for h in range(2):
                        half_send(h, k).start()

        if event in (12, 13, 14, 15):
            weights_far(event - 12)
        if event == Y_AT[2]:
            z_start(1, 0)
            z_start(1, 1)
            zc_copy(0).start()
        for k in range(2):
            if event == Z_AT[k]:
                z_next(1, k)
                if k == 1:
                    z_share(1)

    y_next(1)
    event = 0
    for step in range(1, 5):
        for k in range(2):
            for h in range(2):
                for way in range(2):
                    if x_used(step, way, k):
                        x_copy(step, way, k, h).wait_recv()
                        if step < 4 and x_used(step + 1, way, k):
                            x_copy(step + 1, way, k, h).start()
                after(event)
                event += 1

    load_cos.wait()
    load_sin.wait()

    def turn(v):
        return v * cos_t[...] + pltpu.roll(v, 64, 1) * sin_t[...]

    def new_rows(z):
        return pl.ds(pl.multiple_of(PAST + z * 256, 256), 256)

    def q_src(w, k):
        return sres.at[w, 0, pl.ds(k * 128, 128)]

    def q_dst(k):
        return qb.at[pl.ds(pl.multiple_of(k * 256 + zh * 128, 128), 128)]

    def n_dst():
        return kvb.at[q, new_rows(zh)]

    def q_send(w, k, to):
        return remote(q_src(w, k), q_dst(k), qs.at[w, k], qr.at[k, zh], to)

    def n_send(w, to):
        return remote(sres.at[w, 1], n_dst(), ns.at[w], nr.at[q, zh], to)

    def n_pass(kind, z):
        part = kvb.at[kind, new_rows(z)]
        return remote(part, part, nps.at[kind, z], nr.at[kind, z], sib)

    def project(w):
        out = jnp.dot(xg[...], wb[w], preferred_element_type=F32)
        part_q, part_n = out[:, :HEAD], out[:, HEAD:]
        sres[w, 0] = turn(part_q).astype(BF16)
        sres[w, 1] = jnp.where(q == 0, turn(part_n), part_n).astype(BF16)

    def spread_own(start):
        @pl.when(aligned)
        def _():
            if start:
                for k in range(2):
                    pltpu.make_async_copy(q_src(0, k), q_dst(k), qr.at[k, zh]).start()
                pltpu.make_async_copy(sres.at[0, 1], n_dst(), nr.at[q, zh]).start()

        @pl.when(jnp.logical_not(aligned))
        def _():
            to = functools.partial(dev, y=2 * j + c)
            for copy in (q_send(0, 0, to(c=q)), q_send(0, 1, to(c=q)), n_send(0, to())):
                copy.start() if start else copy.wait_send()

    def spread_other(start):
        to = functools.partial(dev, zh=1 - zh, y=2 * j + c)
        for copy in (q_send(1, 0, to(c=q)), q_send(1, 1, to(c=q)), n_send(1, to())):
            copy.start() if start else copy.wait_send()

    for k in range(4):
        for i in (0, 1, 3, 2):
            w_c(i, k).wait_recv()
    project(1)
    spread_other(True)
    project(0)
    spread_own(True)
    for k in range(2):
        z_next(2, k)
    z_share(2)

    m_s[...] = jnp.full(m_s.shape, NEG, F32)
    l_s[...] = jnp.zeros(l_s.shape, F32)
    acc_s[...] = jnp.zeros(acc_s.shape, F32)

    def q_arrived(g):
        for z in range(2):
            arrived(qb.at[pl.ds(0, 128)], qr.at[g, z])

    def attend(g, first, size, masked):
        keys = kvb[0, pl.ds(first, size), :]
        values = kvb[1, pl.ds(first, size), :]
        rows = pl.ds(g * 256, 256)
        s = lax.dot_general(qb[rows, :], keys, (((1,), (1,)), ((), ())), preferred_element_type=F32)
        if masked:
            n = lax.broadcasted_iota(jnp.int32, (256, 1), 0)
            query = (n // 128) * 256 + (n // 16) % 8 * 32 + g * 16 + n % 16
            n = lax.broadcasted_iota(jnp.int32, (1, size), 1)
            key = (n // 256) * 256 + (n // 16) % 8 * 32 + (n // 128) % 2 * 16 + n % 16
            s = jnp.where(key <= query, s, NEG)
        old = m_s[rows, :]
        new = jnp.maximum(old, jnp.max(s, axis=1, keepdims=True))
        keep = jnp.exp2((old - new) * SCALE2)
        p = jnp.exp2((s - new[:, :1]) * SCALE2)
        l_s[rows, :] = l_s[rows, :] * keep + jnp.sum(p, axis=1, keepdims=True)
        acc_s[rows, :] = acc_s[rows, :] * keep + jnp.dot(p.astype(BF16), values, preferred_element_type=F32)
        m_s[rows, :] = new

    def finish(g):
        rows = pl.ds(g * 256, 256)
        att[rows, :] = (acc_s[rows, :] / l_s[rows, :]).astype(BF16)

    def cached(h, k):
        return pl.multiple_of(h * 2048 + k * 1024, 1024)

    head = zh * 8 + 2 * j + c
    col = pl.ds(pl.multiple_of(head * HEAD, HEAD), HEAD)
    slot_x = pl.ds(pl.multiple_of(x * 16, 16), 16)

    def a_stays(n):
        return jnp.logical_and(n == t, aligned)

    def a_copy(g, n, remotely):
        src = att.at[pl.ds(g * 256 + n * 16, 16)]
        dst = ar.at[g, slot_x, col]
        sem = ar_r.at[g, head]
        if remotely:
            return remote(src, dst, as_.at[g, n], sem, {"tensor": n, "dp": zl * 8 + x * 2 + q})
        return pltpu.make_async_copy(src, dst, sem)

    def a_start(g):
        for n in range(16):

            @pl.when(a_stays(n))
            def _():
                a_copy(g, n, False).start()

            @pl.when(jnp.logical_not(a_stays(n)))
            def _():
                a_copy(g, n, True).start()

    def a_sent(g):
        for n in range(16):

            @pl.when(jnp.logical_not(a_stays(n)))
            def _():
                a_copy(g, n, True).wait_send()

    def a_arrived(g):
        for n in range(16):
            arrived(ar.at[g, pl.ds(0, 16), pl.ds(0, HEAD)], ar_r.at[g, n])

    def ag(g, i):
        part = ar.at[g, slot_x]
        return remote(part, part, ags.at[g, i - 1], agr.at[g, i - 1], dev(x=(x + i) % 4))

    def o_copy(g, i):
        n = (x + i) % 4
        dst = ob.at[pl.ds(g * 16, 16), pl.ds(pl.multiple_of(x * 1024, 1024), 1024)]
        if i == 0:
            return pltpu.make_async_copy(po.at[g, n], dst, ld.at[8 + g])
        return remote(po.at[g, n], dst, os_.at[g, i - 1], or_.at[g, i - 1], dev(x=n))

    def product(g):
        for n in range(4):
            w = jnp.concatenate([wo[n, i].reshape(2048, HEAD) for i in range(2)], axis=1)
            out = jnp.dot(ar[g], w, preferred_element_type=F32).astype(BF16)
            for i in range(4):
                po[g, i, :, n * 256 : (n + 1) * 256] = out[i * 16 : (i + 1) * 16]
        for i in (2, 1, 3, 0):
            o_copy(g, i).start()

    def output(g):
        o_copy(g, 0).wait()
        for i in (1, 3, 2):
            o_copy(g, i).wait_recv()
        rows = pl.ds(g * 16, 16)
        res = (tok[rows, :].astype(F32) + ob[rows, :].astype(F32)).astype(BF16)
        out_o[0, rows, :] = res
        out_o[1, rows, :] = normed(res.astype(F32), gain2[...].astype(F32).reshape(1, WIDTH)).astype(BF16)

    q_arrived(0)
    arrived(cache_h, kfr.at[0])
    for k in range(2):
        arrived(kvb.at[0, pl.ds(0, 1024)], khr.at[k])
        half_pass(k).start()
        attend(0, cached(c, k), 1024, False)
    @pl.when(aligned)
    def _():
        for kind in range(2):
            for z in range(2):
                arrived(kvb.at[0, pl.ds(0, 256)], nr.at[kind, z])
                n_pass(kind, z).start()

    for k in range(2):
        half_pass(k).wait_recv()
        attend(0, cached(1 - c, k), 1024, False)

    @pl.when(jnp.logical_not(aligned))
    def _():
        for kind in range(2):
            for z in range(2):
                arrived(kvb.at[0, pl.ds(0, 256)], nr.at[kind, z])

    attend(0, PAST, BLOCK, True)
    finish(0)
    a_start(0)
    q_arrived(1)
    for n in range(4):
        attend(1, n * 1024, 1024, False)
        if n == 1:
            for k in range(2):
                z_next(3, k)
            z_share(3)
    attend(1, PAST, BLOCK, True)
    finish(1)
    a_start(1)
    for g in range(2):
        a_arrived(g)
        for i in (2, 1, 3):
            ag(g, i).start()
    for k in range(2):
        z_arrived(4, k)
    zc_copy(4).start()
    for i in range(8):
        zc_copy(i).wait_recv()
    load_g2.wait()
    for g in range(2):
        for i in (1, 3, 2):
            ag(g, i).wait_recv()
        product(g)
    for g in range(2):
        output(g)

    for step in range(1, 5):
        for k in range(2):
            for way in range(2):
                if x_used(step, way, k):
                    for h in range(2):
                        x_copy(step, way, k, h).wait_send()
                    z_copy(step, way, k).wait_send()
        for way in range(2):
            y_copy(step, way).wait_send()
    for k in range(4):
        w_z(k).wait_send()
        for i in range(4):
            w_c(i, k).wait_send()
        for way in range(2):
            w_x(way, k).wait_send()
        w_far(k).wait_send()
    for i in range(8):
        zc_copy(i).wait_send()
    for k in range(2):
        half_pass(k).wait_send()
        a_sent(k)
        for i in range(1, 4):
            o_copy(k, i).wait_send()
            ag(k, i).wait_send()

    @pl.when(aligned)
    def _():
        full_send().wait_send()
        for kind in range(2):
            for z in range(2):
                n_pass(kind, z).wait_send()

    @pl.when(jnp.logical_not(aligned))
    def _():
        for k in range(2):
            for h in range(2):
                half_send(h, k).wait_send()

    spread_own(False)
    spread_other(False)


def per_device(tokens, attn_gain, query_weight, key_value_weight, prefix_cache, out_weight, post_gain):
    cosine, sine = rope_tables()
    hbm = pl.BlockSpec(memory_space=pltpu.HBM)
    vmem = pl.BlockSpec(memory_space=pltpu.VMEM)
    dma = pltpu.SemaphoreType.DMA
    rows = jax.ShapeDtypeStruct((2, *tokens.shape), BF16)
    out = pl.pallas_call(
        kernel,
        out_shape=rows,
        in_specs=[hbm] * 9,
        out_specs=vmem,
        scratch_shapes=[
            pltpu.VMEM((32, WIDTH), BF16),
            pltpu.VMEM((WIDTH,), BF16),
            pltpu.VMEM((WIDTH,), BF16),
            pltpu.VMEM((256, WIDTH), BF16),
            pltpu.VMEM((2, WIDTH, 256), BF16),
            pltpu.VMEM((256, HEAD), F32),
            pltpu.VMEM((256, HEAD), F32),
            pltpu.VMEM((2, 2, 256, HEAD), BF16),
            pltpu.VMEM((BLOCK, HEAD), BF16),
            pltpu.VMEM((2, PAST + BLOCK, HEAD), BF16),
            pltpu.VMEM((4, 2, 2, 8, HEAD, HEAD), BF16),
            pltpu.VMEM((BLOCK, HEAD), BF16),
            pltpu.VMEM((2, 64, 2048), BF16),
            pltpu.VMEM((2, 4, 16, 1024), BF16),
            pltpu.VMEM((32, WIDTH), BF16),
            pltpu.VMEM((BLOCK, HEAD), F32),
            pltpu.VMEM((BLOCK, HEAD), F32),
            pltpu.VMEM((BLOCK, HEAD), F32),
            dma((10,)),
            dma((2, 4, 2, 2)), dma((2, 4, 2, 2)),
            dma((2, 4)), dma((2, 4)),
            dma((4,)), dma((4,)),
            dma((3, 4)), dma((3, 4)),
            dma((4, 4)), dma((4, 4)),
            dma((1,)), dma((1,)),
            dma((2, 2)), dma((2,)),
            dma((2,)), dma((2,)),
            dma((2, 2)), dma((2, 2)),
            dma((2,)), dma((2, 2)), dma((2, 2)),
            dma((2, 4, 2)), dma((2, 4, 2)),
            dma((8,)), dma((8,)),
            dma((2, 16)), dma((2, 16)),
            dma((2, 3)), dma((2, 3)),
            dma((2, 3)), dma((2, 3)),
        ],
        compiler_params=pltpu.CompilerParams(
            collective_id=0, has_side_effects=True, vmem_limit_bytes=60 * 2**20
        ),
        name="sublayer",
    )(
        tokens, attn_gain, query_weight, key_value_weight, prefix_cache,
        out_weight, post_gain, jnp.asarray(cosine), jnp.asarray(sine),
    )
    return out[0], out[1]

def solution(mesh):
    rows = P(("dp", "tensor"), None)
    return jax.shard_map(
        per_device,
        mesh=mesh,
        in_specs=(rows, P(), P(None, "tensor"), P(None, "tensor"), P("dp", "tensor"), P("tensor", None), P()),
        out_specs=(rows, rows),
        check_vma=False,
    )
```

time: 91.6 us -> 83 us (0.906)
  Pallas kernels: 88 us -> 80.3 us
  other arithmetic: 2.69 us -> 0 us
  local copies, waits for them, and re-layouts: 0.01 us -> 1.85 us
    pallas_call x1, Pallas kernels: 88 us -> 80.3 us  [per_device(): pl.pallas_call(kernel, out_shape=rows, in_specs=[hbm] * 9, out_specs=vmem...]
    squeeze x0 -> x1, local copies, waits for them, and re-layouts: none -> 1.85 us  [per_device(): return (out[0], out[1])]
    convert_element_type x2 -> x0, other arithmetic: 1.53 us -> none  [the longest x1 0.83 us: per_device(): return (residual_out, normed(residual_out.astype(F32), gain).astype(BF16))]
    reduce_sum x1 -> x0, other arithmetic: 1.15 us -> none  [normed(): mean_square = jnp.mean(rows * rows, axis=-1, keepdims=True)]
where the time goes in v3:
time: 83 us; the launch traced here: 82.8 us
  Pallas kernels  80.3 us (97%)
  local copies, waits for them, and re-layouts  1.85 us (2%)
    pallas_call x1, Pallas kernels, per_device(): pl.pallas_call(kernel, out_shape=rows, in_specs=[hbm] * 9, out_specs=vmem...  80.3 us
    squeeze x1, local copies, waits for them, and re-layouts, per_device(): return (out[0], out[1])  1.85 us

profile of v3, /device:TPU:1, one launch (start us, length us, event | category | flops | bytes accessed | tf_op | source)
XLA Modules:
  0.0 82.8 jit_solution(7546401234966490751)
XLA Ops:
  0.6 80.3 %sublayer.1 = bf16[2,32,4096]{2,1,0:T(8,128)(2,1)} custom-call(bf16[32,4096]{1,0:T(8,128)(2,1)} %tok_h.1, bf16[4096]{0:T(1024)(128)(2,1)} %gain1_h.1, bf16[4096,128]{1,0:T(8,128)(2,1)} %wq_h.1, bf16[4096,128]{1,0:T(8,128)(2,1)} %wkv_h.1, bf16[4096,128]{1,0:T(8,128)(2,1)} %cache_h.1, bf16[128,4096]{1,0:T(8,128)(2,1)} %wout_h.1, bf16[4096]{0:T(1024)(128)(2,1)} %gain2_h.1, ...), custom_call_target="tpu_custom_call" | custom-call | tf_op jit(solution)/shard_map/sublayer/pallas_call | solution.py:547
  80.9 1.9 %slice_bitcast_fusion = (bf16[32,4096]{1,0:T(8,128)(2,1)}, bf16[32,4096]{1,0:T(8,128)(2,1)}) fusion(bf16[2,32,4096]{2,1,0:T(8,128)(2,1)} %sublayer.1), kind=kLoop, calls=%fused_computation | loop fusion | bytes 1048576 | tf_op jit(solution)/shard_map/squeeze | solution.py:596

commit v4 on v3

--- a/solution.py
+++ b/solution.py
@@ -246,13 +246,12 @@
             weights_in()
         if event in (8, 9, 10, 11):
             weights_on(event - 8)
-        if event == 11:
+        if event in (11, 15):
 
             @pl.when(jnp.logical_not(aligned))
             def _():
-                for k in range(2):
-                    for h in range(2):
-                        half_send(h, k).start()
+                for h in range(2):
+                    half_send(h, (event - 11) // 4).start()
 
         if event in (12, 13, 14, 15):
             weights_far(event - 12)
@@ -472,7 +471,7 @@
     q_arrived(1)
     for n in range(4):
         attend(1, n * 1024, 1024, False)
-        if n == 1:
+        if n == 0:
             for k in range(2):
                 z_next(3, k)
             z_share(3)

time: 83 us -> 83 us (level)
  no operation moved by 1% of the time
where the time goes in v4:
time: 83 us; the launch traced here: 82.7 us
  Pallas kernels  80.2 us (97%)
  local copies, waits for them, and re-layouts  1.85 us (2%)
    pallas_call x1, Pallas kernels, per_device(): pl.pallas_call(kernel, out_shape=rows, in_specs=[hbm] * 9, out_specs=vmem...  80.2 us
    squeeze x1, local copies, waits for them, and re-layouts, per_device(): return (out[0], out[1])  1.85 us

profile of v4, /device:TPU:1, one launch (start us, length us, event | category | flops | bytes accessed | tf_op | source)
XLA Modules:
  0.0 82.7 jit_solution(9684551893703363915)
XLA Ops:
  0.6 80.2 %sublayer.1 = bf16[2,32,4096]{2,1,0:T(8,128)(2,1)} custom-call(bf16[32,4096]{1,0:T(8,128)(2,1)} %tok_h.1, bf16[4096]{0:T(1024)(128)(2,1)} %gain1_h.1, bf16[4096,128]{1,0:T(8,128)(2,1)} %wq_h.1, bf16[4096,128]{1,0:T(8,128)(2,1)} %wkv_h.1, bf16[4096,128]{1,0:T(8,128)(2,1)} %cache_h.1, bf16[128,4096]{1,0:T(8,128)(2,1)} %wout_h.1, bf16[4096]{0:T(1024)(128)(2,1)} %gain2_h.1, ...), custom_call_target="tpu_custom_call" | custom-call | tf_op jit(solution)/shard_map/sublayer/pallas_call | solution.py:546
  80.8 1.9 %slice_bitcast_fusion = (bf16[32,4096]{1,0:T(8,128)(2,1)}, bf16[32,4096]{1,0:T(8,128)(2,1)}) fusion(bf16[2,32,4096]{2,1,0:T(8,128)(2,1)} %sublayer.1), kind=kLoop, calls=%fused_computation | loop fusion | bytes 1048576 | tf_op jit(solution)/shard_map/squeeze | solution.py:595
